TPU v7x, 32 devices: a whole 2x2x4 slice. The times are simulated.
32 devices in a mesh: row: 4 (over y, x), col: 8 (over z, core).
Axes of the slice: x: 2, y: 2, z: 4, core: 2. Of those that a mesh axis runs over, the one named last changes fastest.
Arguments:
- velocity: float32 [3, 128, 384, 1024], P(None, 'col', 'row'), may hold values from -6 to 6
- x_operator: float32 [1024, 1024], replicated, may hold values from -0.1875 to 0.1875
- y_operator: float32 [384, 384], replicated, may hold values from -0.3125 to 0.3125
- z_operator: float32 [128, 128], replicated, may hold values from -0.5 to 0.5
- y_metric: float32 [384], replicated, may hold values from 0.5 to 4
Outputs:
- grads: bfloat16 [9, 128, 384, 1024], P(None, None, 'col', 'row')
All inputs are finite; a program needn't handle non-finite values.
Results may differ from a plain program's by a relative error of at most 0.0095.
Values may be sent and summed in bfloat16 or wider, within the bound.
A program may use at most 192 MiB of HBM per device.

v0:
```python
import jax
import jax.numpy as jnp
from jax import lax
from jax.sharding import PartitionSpec as P

HIGHEST = lax.Precision.HIGHEST


def shards(velocity, x_operator, y_operator, z_operator, y_metric):
    along_x = jnp.einsum("czyx,xw->czyw", velocity, x_operator, precision=HIGHEST).astype(
        jnp.bfloat16
    )
    y_pencil = lax.all_to_all(
        velocity.astype(jnp.bfloat16), "row", split_axis=3, concat_axis=2, tiled=True
    ).astype(velocity.dtype)
    xderiv_y = lax.all_to_all(along_x, "row", split_axis=3, concat_axis=2, tiled=True)
    along_y = (
        jnp.einsum("czyx,yw->czwx", y_pencil, y_operator, precision=HIGHEST)
        * y_metric[None, None, :, None]
    ).astype(jnp.bfloat16)
    z_pencil = lax.all_to_all(
        y_pencil.astype(jnp.bfloat16), "col", split_axis=2, concat_axis=1, tiled=True
    ).astype(y_pencil.dtype)
    planes = jnp.stack([xderiv_y, along_y], axis=1)
    planes_z = lax.all_to_all(planes, "col", split_axis=3, concat_axis=2, tiled=True)
    along_z = jnp.einsum("czyx,zw->cwyx", z_pencil, z_operator, precision=HIGHEST).astype(
        jnp.bfloat16
    )
    gradients = jnp.concatenate([planes_z, along_z[:, None]], axis=1)
    shape_now = gradients.shape
    return gradients.reshape(9, shape_now[2], shape_now[3], shape_now[4])


def solution(mesh):
    return jax.shard_map(
        shards,
        mesh=mesh,
        in_specs=(P(None, "col", "row", None), P(), P(), P(), P()),
        out_specs=P(None, None, "col", "row"),
        check_vma=False,
    )
```

profile of v0, /device:TPU:9, one launch (start us, length us, event | category | flops | bytes accessed | tf_op | source)
XLA Modules:
  0.0 975.8 jit_solution(12452609262772497414)
XLA Ops:
  0.0 10.1 %convert_element_type.22 = bf16[3,16,96,1024]{3,2,1,0:T(8,128)(2,1)} convert(f32[3,16,96,1024]{3,2,1,0:T(8,128)} %param.5) | non-fusion elementwise | flops 4718592 | bytes 28311552 | tf_op jit(solution)/shard_map/convert_element_type | solution.py:14
  10.1 15.9 %copy.43 = bf16[3,16,96,1024]{2,1,0,3:T(8,128)(2,1)} copy(bf16[3,16,96,1024]{3,2,1,0:T(8,128)(2,1)} %convert_element_type.22) | data formatting | bytes 18874368 | tf_op jit(solution)/shard_map/convert_element_type | solution.py:14
  26.0 6.3 all-to-all-start.1
  32.3 66.8 %convolution_convert_fusion = bf16[3,16,96,1024]{3,2,1,0:T(8,128)(2,1)} fusion(f32[3,16,96,1024]{3,2,1,0:T(8,128)} %param.5, f32[1024,1024]{1,0:T(8,128)} %param.6), kind=kOutput, calls=%fused_computation.5 | convolution fusion | flops 57986777088 | bytes 32505856 | tf_op jit(solution)/shard_map/czyx,xw->czyw/dot_general | solution.py:10
  99.1 15.8 %copy.41 = bf16[3,16,96,1024]{2,1,0,3:T(8,128)(2,1)} copy(bf16[3,16,96,1024]{3,2,1,0:T(8,128)(2,1)} %convolution_convert_fusion) | data formatting | bytes 18874368 | tf_op jit(solution)/shard_map/convert_element_type | solution.py:10
  114.9 54.2 %all-to-all-done.1 = bf16[3,16,96,1024]{2,1,0,3:T(8,128)(2,1)} async-done(((bf16[3,16,96,1024]{2,1,0,3:T(8,128)(2,1)}), bf16[3,16,96,1024]{2,1,0,3:T(8,128)(2,1)}, u32[]{:S(2)}, u32[]{:S(2)}) %all-to-all-start.1) | async-done | bytes 9437216 | tf_op jit(solution)/shard_map/all_to_all | solution.py:13
  169.1 6.3 all-to-all-start
  175.4 17.3 %copy.59 = bf16[3,16,96,4,256]{4,1,0,2,3:T(8,128)(2,1)} copy(bf16[3,16,96,4,256]{2,1,0,4,3:T(8,128)(2,1)} %bitcast.6) | data formatting | bytes 18874368 | tf_op jit(solution)/shard_map/all_to_all | solution.py:13
  192.6 119.5 %all-to-all-done = bf16[3,16,96,1024]{2,1,0,3:T(8,128)(2,1)} async-done(((bf16[3,16,96,1024]{2,1,0,3:T(8,128)(2,1)}), bf16[3,16,96,1024]{2,1,0,3:T(8,128)(2,1)}, u32[]{:S(2)}, u32[]{:S(2)}) %all-to-all-start) | async-done | bytes 9437216 | tf_op jit(solution)/shard_map/all_to_all | solution.py:16
  312.1 6.7 all-to-all-start.3
  318.8 15.6 %copy.44 = bf16[3,16,96,4,256]{4,2,3,1,0:T(8,128)(2,1)} copy(bf16[3,16,96,4,256]{2,1,0,4,3:T(8,128)(2,1)} %bitcast.6) | data formatting | bytes 18874368 | tf_op jit(solution)/shard_map/all_to_all | solution.py:13
  334.4 15.9 %copy.42 = bf16[3,16,96,4,256]{4,2,3,1,0:T(8,128)(2,1)} copy(bf16[3,16,96,4,256]{2,1,0,4,3:T(8,128)(2,1)} %bitcast.2) | data formatting | bytes 18874368 | tf_op jit(solution)/shard_map/all_to_all | solution.py:16
  350.3 0.0 copy-done.4
  350.3 17.4 %fusion = bf16[3,1,16,384,256]{4,3,2,0,1:T(8,128)(2,1)S(1)} fusion(f32[384]{0:T(512)S(1)} %copy-done.4, bf16[3,16,384,256]{3,2,1,0:T(8,128)(2,1)} %bitcast.44, f32[384,384]{1,0:T(8,128)S(1)} %copy-done), kind=kOutput, calls=%fused_computation.3 | convolution fusion | flops 21752709120 | bytes 19465728 | tf_op jit(solution)/shard_map/czyx,yw->czwx/dot_general | solution.py:18
  367.8 1.9 pad_maximum_fusion.1
  369.7 34.9 %copy.46 = bf16[3,2,16,384,256]{4,2,0,1,3:T(8,128)(2,1)} copy(bf16[3,2,16,384,256]{4,3,2,0,1:T(8,128)(2,1)S(1)} %pad_maximum_fusion.1) | data formatting | bytes 37748736 | tf_op jit(solution)/shard_map/stack | solution.py:24
  404.5 117.1 %all-to-all-done.3 = bf16[3,16,384,256]{3,1,0,2:T(8,128)(2,1)} async-done(((bf16[3,16,384,256]{3,1,0,2:T(8,128)(2,1)}), bf16[3,16,384,256]{3,1,0,2:T(8,128)(2,1)}, u32[]{:S(2)}, u32[]{:S(2)}) %all-to-all-start.3) | async-done | bytes 9437216 | tf_op jit(solution)/shard_map/all_to_all | solution.py:21
  521.6 9.5 all-to-all-start.2
  531.1 8.8 copy.50
  539.9 12.6 %convert_bitcast_fusion = bf16[3,1,128,48,256]{4,2,3,0,1:T(8,128)(2,1)} fusion(bf16[3,128,48,256]{3,1,2,0:T(8,128)(2,1)} %bitcast.41, f32[128,128]{1,0:T(8,128)S(1)} %copy-done.3), kind=kOutput, calls=%fused_computation.4 | convolution fusion | flops 7252475904 | bytes 18939904 | tf_op jit(solution)/shard_map/czyx,zw->cwyx/dot_general | solution.py:26
  552.5 12.8 %copy.52 = bf16[3,1,128,48,256]{4,3,2,1,0:T(8,128)(2,1)} copy(bf16[3,1,128,48,256]{4,2,3,0,1:T(8,128)(2,1)} %convert_bitcast_fusion) | data formatting | bytes 18874368 | tf_op jit(solution)/shard_map/broadcast_in_dim | solution.py:29
  565.3 370.8 %all-to-all-done.2 = bf16[3,2,16,384,256]{4,2,0,1,3:T(8,128)(2,1)} async-done(((bf16[3,2,16,384,256]{4,2,0,1,3:T(8,128)(2,1)}), bf16[3,2,16,384,256]{4,2,0,1,3:T(8,128)(2,1)}, u32[]{:S(2)}, u32[]{:S(2)}) %all-to-all-start.2) | async-done | bytes 18874400 | tf_op jit(solution)/shard_map/all_to_all | solution.py:25
  936.1 20.1 %copy.48 = bf16[3,2,8,16,48,256]{5,4,3,2,1,0:T(8,128)(2,1)} copy(bf16[3,2,8,16,48,256]{5,3,0,1,4,2:T(8,128)(2,1)} %bitcast.13) | data formatting | bytes 37748736 | tf_op jit(solution)/shard_map/all_to_all | solution.py:25
  956.2 19.5 %pad_maximum_fusion = bf16[3,3,128,48,256]{4,3,2,1,0:T(8,128)(2,1)} fusion(bf16[3,1,128,48,256]{4,3,2,1,0:T(8,128)(2,1)} %copy.52, bf16[3,2,128,48,256]{4,3,2,1,0:T(8,128)(2,1)} %bitcast.40), kind=kLoop, calls=%fused_computation | loop fusion | flops 14155776 | bytes 56623104 | tf_op jit(solution)/shard_map/concatenate | solution.py:29
  (9 shorter events, 0.0 us)
Async XLA Ops:
  0.0 350.3 %copy-start = (f32[384,384]{1,0:T(8,128)S(1)}, f32[384,384]{1,0:T(8,128)}, u32[]{:S(2)}) copy-start(f32[384,384]{1,0:T(8,128)} %param.7) | copy-start | bytes 1769476
  26.0 143.1 %all-to-all-start.1 = ((bf16[3,16,96,1024]{2,1,0,3:T(8,128)(2,1)}), bf16[3,16,96,1024]{2,1,0,3:T(8,128)(2,1)}, u32[]{:S(2)}, u32[]{:S(2)}) async-start(bf16[3,16,96,1024]{2,1,0,3:T(8,128)(2,1)} %copy.43), calls=%async_computation.1 | async-start | bytes 25165824 | tf_op jit(solution)/shard_map/all_to_all | solution.py:13
  169.1 143.0 %all-to-all-start = ((bf16[3,16,96,1024]{2,1,0,3:T(8,128)(2,1)}), bf16[3,16,96,1024]{2,1,0,3:T(8,128)(2,1)}, u32[]{:S(2)}, u32[]{:S(2)}) async-start(bf16[3,16,96,1024]{2,1,0,3:T(8,128)(2,1)} %copy.41), calls=%async_computation | async-start | bytes 25165824 | tf_op jit(solution)/shard_map/all_to_all | solution.py:16
  312.1 209.5 %all-to-all-start.3 = ((bf16[3,16,384,256]{3,1,0,2:T(8,128)(2,1)}), bf16[3,16,384,256]{3,1,0,2:T(8,128)(2,1)}, u32[]{:S(2)}, u32[]{:S(2)}) async-start(bf16[3,16,384,256]{3,1,0,2:T(8,128)(2,1)} %bitcast.42), calls=%async_computation.3 | async-start | bytes 18874368 | tf_op jit(solution)/shard_map/all_to_all | solution.py:21
  334.4 15.9 %copy-start.4 = (f32[384]{0:T(512)S(1)}, f32[384]{0:T(512)}, u32[]{:S(2)}) copy-start(f32[384]{0:T(512)} %param.9) | copy-start | bytes 4612
  350.3 17.4 %copy-start.2 = (bf16[3,16,96,4,256]{4,2,3,1,0:T(8,128)(2,1)S(1)}, bf16[3,16,96,4,256]{4,2,3,1,0:T(8,128)(2,1)}, u32[]{:S(2)}) copy-start(bf16[3,16,96,4,256]{4,2,3,1,0:T(8,128)(2,1)} %copy.42) | copy-start | bytes 28311556
  521.6 414.5 %all-to-all-start.2 = ((bf16[3,2,16,384,256]{4,2,0,1,3:T(8,128)(2,1)}), bf16[3,2,16,384,256]{4,2,0,1,3:T(8,128)(2,1)}, u32[]{:S(2)}, u32[]{:S(2)}) async-start(bf16[3,2,16,384,256]{4,2,0,1,3:T(8,128)(2,1)} %copy.46), calls=%async_computation.2 | async-start | bytes 37748736 | tf_op jit(solution)/shard_map/all_to_all | solution.py:25
  531.1 8.8 copy-start.3
  956.2 19.5 %copy-start.1 = (f32[384,384]{1,0:T(8,128)S(1)}, f32[384,384]{1,0:T(8,128)}, u32[]{:S(2)}) copy-start(f32[384,384]{1,0:T(8,128)} %param.7) | copy-start | bytes 1769476
where the time goes:
time: 983 us; the launch traced here: 976 us
  waiting for transfers between devices  662 us (67%)
  local copies, waits for them, and re-layouts  157 us (16%)
  matrix products  96.8 us (10%)
  other arithmetic  31.5 us (3%)
  starting transfers between devices  28.8 us (3%)
    all_to_all x1, waiting for transfers between devices, shards(): lax.all_to_all(planes, 'col', split_axis=3, concat_axis=2, tiled=True)  371 us
    all_to_all x1, waiting for transfers between devices, shards(): lax.all_to_all(along_x, 'row', split_axis=3, concat_axis=2, tiled=True)  119 us
    all_to_all x1, waiting for transfers between devices, shards(): lax.all_to_all(y_pencil.astype(jnp.bfloat16), 'col', split_axis=2, concat...  117 us
    dot_general x1, matrix products, shards(): jnp.einsum('czyx,xw->czyw', velocity, x_operator, precision=HIGHEST)  66.8 us
    all_to_all x1, waiting for transfers between devices, shards(): lax.all_to_all(velocity.astype(jnp.bfloat16), 'row', split_axis=3, concat...  54.2 us
    another operation x1, local copies, waits for them, and re-layouts, shards(): planes = jnp.stack([xderiv_y, along_y], axis=1)  34.9 us
    all_to_all x2, local copies, waits for them, and re-layouts, shards(): lax.all_to_all(velocity.astype(jnp.bfloat16), 'row', split_axis=3, concat...  32.9 us
    all_to_all x1, local copies, waits for them, and re-layouts, shards(): lax.all_to_all(planes, 'col', split_axis=3, concat_axis=2, tiled=True)  20.1 us
  transfers between devices with their start and end apart: 4, of which 4 were waited for; matrix products, arithmetic and copies ran while one was open for 23% of the time, Pallas kernels for 0%

commit v1 on v0

v1 whole, which is shorter than its diff:
```python
import functools

import jax
import jax.numpy as jnp
from jax import lax
from jax.experimental import pallas as pl
from jax.experimental.pallas import tpu as pltpu
from jax.sharding import PartitionSpec as P

MESH = pl.DeviceIdType.MESH
HALVES = 2


def kernel(
    rows, cols, halves, yop_ref, xop_ref, v_ref, vz_ref, gx_ref, gy_ref,
    ypen, ay, xpen, ax,
    row_v_s, row_v_r, col_v_s, col_v_r, col_y_s, col_y_r, row_f_s, row_f_r, row_x_s, row_x_r, own_sem,
):
    r, c = lax.axis_index("row"), lax.axis_index("col")
    k = cols // rows
    chunks, _, zh, yc, xb = ypen.shape
    ny = cols * yc

    barrier = pltpu.get_barrier_semaphore()
    for d in range(1, rows):
        pl.semaphore_signal(barrier, inc=1, device_id=(lax.rem(r + d, rows), c), device_id_type=MESH)
    for d in range(1, cols):
        pl.semaphore_signal(barrier, inc=1, device_id=(r, lax.rem(c + d, cols)), device_id_type=MESH)
    pl.semaphore_wait(barrier, rows + cols - 2)

    def place(q):
        return q // halves, pl.ds((q % halves) * zh, zh)

    def remote(src, dst, send, recv, target):
        return pltpu.make_async_remote_copy(
            src_ref=src, dst_ref=dst, send_sem=send, recv_sem=recv, device_id=target, device_id_type=MESH
        )

    def row_v(q):
        comp, zs = place(q)
        def src(t):
            return v_ref.at[comp, :, zs, :, pl.ds(pl.multiple_of(t * xb, 128), xb)]
        dst = ypen.at[q, pl.ds(r * k, k)]
        others = []
        for d in range(1, rows):
            t = lax.rem(r + d, rows)
            others.append(remote(src(t), dst, row_v_s.at[q, d - 1], row_v_r.at[q, d - 1], (t, c)))
        return others, pltpu.make_async_copy(src(r), dst, own_sem.at[0, q])

    def col_family(q, source, result, send, recv, own):
        comp, zs = place(q)
        dst = result.at[comp, c, zs]
        others = []
        for d in range(1, cols):
            t = lax.rem(c + d, cols)
            others.append(remote(source.at[q, t], dst, send.at[q, d - 1], recv.at[q, d - 1], (r, t)))
        return others, pltpu.make_async_copy(source.at[q, c], dst, own_sem.at[own, q])

    def col_v(q):
        return col_family(q, ypen, vz_ref, col_v_s, col_v_r, 1)

    def col_y(q):
        return col_family(q, ay, gy_ref, col_y_s, col_y_r, 2)

    def row_f(q):
        comp, zs = place(q)
        def src(t):
            return vz_ref.at[comp, pl.ds(t * k, k), zs]
        dst = xpen.at[q, r]
        others = []
        for d in range(1, rows):
            t = lax.rem(r + d, rows)
            others.append(remote(src(t), dst, row_f_s.at[q, d - 1], row_f_r.at[q, d - 1], (t, c)))
        return others, pltpu.make_async_copy(src(r), dst, own_sem.at[3, q])

    def row_x(q):
        comp, zs = place(q)
        dst = gx_ref.at[comp, pl.ds(r * k, k), zs]
        others = []
        for d in range(1, rows):
            t = lax.rem(r + d, rows)
            others.append(remote(ax.at[q, t], dst, row_x_s.at[q, d - 1], row_x_r.at[q, d - 1], (t, c)))
        return others, pltpu.make_async_copy(ax.at[q, r], dst, own_sem.at[4, q])

    def start(family, q):
        others, own = family(q)
        for copy in others:
            copy.start()
        own.start()

    def arrived(family, q):
        others, own = family(q)
        for copy in others:
            copy.wait_recv()
        own.wait()

    def sent(family, q):
        for copy in family(q)[0]:
            copy.wait_send()

    def flat(x, width):
        if yc % 16:
            return x.astype(jnp.float32).reshape(-1, width).astype(x.dtype)
        return x.reshape(-1, width)

    def along_y(q):
        @pl.loop(0, zh)
        def _(z):
            field = flat(ypen[q, :, z], xb)
            product = jnp.dot(yop_ref[...], field, preferred_element_type=jnp.float32)
            ay[q, :, z] = product.reshape(cols, yc, xb).astype(ay.dtype)

    def along_x(q):
        for part in range(k):
            field = jnp.concatenate([flat(xpen[q, j, part], xb) for j in range(rows)], axis=1)

            @pl.loop(0, rows)
            def _(w):
                product = jnp.dot(field, xop_ref[w], preferred_element_type=jnp.float32)
                ax[q, w, part] = product.reshape(zh, yc, xb).astype(ax.dtype)

    @pl.loop(0, chunks)
    def _(q):
        start(row_v, q)

    @pl.loop(0, chunks)
    def _(q):
        arrived(row_v, q)
        start(col_v, q)
        along_y(q)

    def finish_x(q):
        arrived(row_f, q)
        along_x(q)
        start(row_x, q)

    @pl.loop(0, chunks)
    def _(q):
        arrived(col_v, q)
        start(row_f, q)
        start(col_y, q)

        @pl.when(q > 0)
        def _():
            finish_x(q - 1)

    finish_x(chunks - 1)

    @pl.loop(0, chunks)
    def _(q):
        arrived(row_x, q)
        arrived(col_y, q)
        for family in (row_v, col_v, col_y, row_f, row_x):
            sent(family, q)


def shards(rows, cols, velocity, x_operator, y_operator, z_operator, y_metric):
    bf16 = jnp.bfloat16
    comps, zb, yb, nx = velocity.shape
    k = cols // rows
    yc, xb, ny = yb // k, nx // rows, yb * rows
    halves = HALVES
    zh, chunks = zb // halves, comps * halves

    v = velocity.astype(bf16).reshape(comps, zb, k, yc, nx).transpose(0, 2, 1, 3, 4)
    yop = (y_operator * y_metric[None, :]).T.astype(bf16)
    xop = x_operator.astype(bf16).reshape(nx, rows, xb).transpose(1, 0, 2)

    final = jax.ShapeDtypeStruct((comps, cols, zb, yc, xb), bf16)
    pencils = pltpu.VMEM((chunks, cols, zh, yc, xb), bf16)
    blocks = pltpu.VMEM((chunks, rows, k, zh, yc, xb), bf16)
    row_sem = pltpu.SemaphoreType.DMA((chunks, rows - 1))
    col_sem = pltpu.SemaphoreType.DMA((chunks, cols - 1))
    work = comps * zb * yb * nx
    vz, gx, gy = pl.pallas_call(
        functools.partial(kernel, rows, cols, halves),
        out_shape=[final] * 3,
        in_specs=[pl.BlockSpec(memory_space=pltpu.VMEM)] * 2 + [pl.BlockSpec(memory_space=pl.ANY)],
        out_specs=[pl.BlockSpec(memory_space=pl.ANY)] * 3,
        scratch_shapes=[
            pencils, pencils, blocks, blocks,
            row_sem, row_sem, col_sem, col_sem, col_sem, col_sem, row_sem, row_sem, row_sem, row_sem,
            pltpu.SemaphoreType.DMA((5, chunks)),
        ],
        cost_estimate=pl.CostEstimate(flops=2 * work * (nx + ny), bytes_accessed=10 * work, transcendentals=0),
        compiler_params=pltpu.CompilerParams(
            collective_id=0, has_side_effects=True, vmem_limit_bytes=56 * 2**20
        ),
    )(yop, xop, v)

    vz, gx, gy = (a.reshape(comps, cols * zb, yc, xb) for a in (vz, gx, gy))
    gz = jnp.einsum(
        "czyx,zw->cwyx", vz, z_operator.astype(bf16), preferred_element_type=jnp.float32
    ).astype(bf16)
    return jnp.stack([gx, gy, gz], axis=1).reshape(3 * comps, cols * zb, yc, xb)


def solution(mesh):
    return jax.shard_map(
        functools.partial(shards, mesh.shape["row"], mesh.shape["col"]),
        mesh=mesh,
        in_specs=(P(None, "col", "row", None), P(), P(), P(), P()),
        out_specs=P(None, None, "col", "row"),
        check_vma=False,
    )
```

time: 983 us -> 557 us (0.57)
  waiting for transfers between devices: 662 us -> 0 us
  Pallas kernels: 0 us -> 433 us
  matrix products: 96.8 us -> 9.77 us
  local copies, waits for them, and re-layouts: 157 us -> 81.4 us
  starting transfers between devices: 28.8 us -> 0 us
    all_to_all x4 -> x0, waiting for transfers between devices: 662 us -> none  [the longest x1 371 us: shards(): lax.all_to_all(planes, 'col', split_axis=3, concat_axis=2, tiled=True)]
    pallas_call x0 -> x1, Pallas kernels: none -> 433 us  [shards(): pl.pallas_call(functools.partial(kernel, rows, cols, halves), out_shape=[...]
    dot_general x3 -> x1, matrix products: 96.8 us -> 9.77 us  [shards(): jnp.einsum('czyx,zw->cwyx', vz, z_operator.astype(bf16), preferred_elemen...]
    all_to_all x5 -> x0, local copies, waits for them, and re-layouts: 77.7 us -> none  [the longest x2 32.9 us: shards(): lax.all_to_all(velocity.astype(jnp.bfloat16), 'row', split_axis=3, concat...]
    convert_element_type x2 -> x0, local copies, waits for them, and re-layouts: 31.7 us -> none  [the longest x1 15.9 us: shards(): velocity.astype(jnp.bfloat16)]
    another operation x1 -> x3, local copies, waits for them, and re-layouts: 34.9 us -> 64.8 us  [shards(): return jnp.stack([gx, gy, gz], axis=1).reshape(3 * comps, cols * zb, yc, xb)]
    all_to_all x4 -> x0, starting transfers between devices: 28.8 us -> none  [the longest x1 9.49 us: shards(): lax.all_to_all(planes, 'col', split_axis=3, concat_axis=2, tiled=True)]
    concatenate x1 -> x0, other arithmetic: 19.5 us -> none  [shards(): gradients = jnp.concatenate([planes_z, along_z[:, None]], axis=1)]
  transfers between devices with their start and end apart: 4 -> 0, of which waited for: 4 -> 0; matrix products, arithmetic and copies ran while one was open for 23% -> 0% of each run, Pallas kernels for 0% -> 0%
where the time goes in v1:
time: 557 us; the launch traced here: 555 us
  Pallas kernels  433 us (78%)
  local copies, waits for them, and re-layouts  81.4 us (15%)
  other arithmetic  31.1 us (6%)
  matrix products  9.77 us (2%)
    pallas_call x1, Pallas kernels, shards(): pl.pallas_call(functools.partial(kernel, rows, cols, halves), out_shape=[...  433 us
    another operation x3, local copies, waits for them, and re-layouts, shards(): return jnp.stack([gx, gy, gz], axis=1).reshape(3 * comps, cols * zb, yc, xb)  64.8 us
    another operation x1, other arithmetic, shards(): return jnp.stack([gx, gy, gz], axis=1).reshape(3 * comps, cols * zb, yc, xb)  19.6 us

profile of v1, /device:TPU:9, one launch (start us, length us, event | category | flops | bytes accessed | tf_op | source)
XLA Modules:
  0.0 554.9 jit_solution(13082595053088224679)
XLA Ops:
  0.0 1.3 copy.10
  1.3 1.5 fusion.4.yop_ref
  2.8 3.3 copy.11
  6.2 2.5 copy.12
  8.7 9.9 %convert_element_type.23 = bf16[3,16,96,1024]{3,2,1,0:T(8,128)(2,1)} convert(f32[3,16,96,1024]{3,2,1,0:T(8,128)} %param.5) | non-fusion elementwise | flops 4718592 | bytes 28311552 | tf_op jit(solution)/shard_map/convert_element_type | solution.py:165
  18.6 9.4 %copy.24 = bf16[3,16,2,48,1024]{4,3,1,2,0:T(8,128)(2,1)} copy(bf16[3,16,2,48,1024]{4,3,2,1,0:T(8,128)(2,1)} %bitcast.21) | data formatting | bytes 18874368 | tf_op jit(solution)/shard_map/reshape | solution.py:165
  28.0 432.6 %shard_map.55 = (bf16[3,8,16,48,256]{4,3,2,1,0:T(8,128)(2,1)}, bf16[3,8,16,48,256]{4,3,2,1,0:T(8,128)(2,1)}, bf16[3,8,16,48,256]{4,3,2,1,0:T(8,128)(2,1)}) custom-call(bf16[384,384]{1,0:T(8,128)(2,1)} %fusion.4.yop_ref, bf16[4,1024,256]{2,1,0:T(8,128)(2,1)} %bitcast.27, bf16[3,2,16,48,1024]{4,3,2,1,0:T(8,128)(2,1)} %bitcast.24), custom_call_target="tpu_custom_call" | custom-call | flops 13287555072 | bytes 47185920 | tf_op jit(solution)/shard_map/pallas_call | solution.py:175
  460.7 13.3 %copy.15 = bf16[3,1,128,48,256]{2,4,3,0,1:T(8,128)(2,1)} copy(bf16[3,1,128,48,256]{4,3,2,0,1:T(8,128)(2,1)} %bitcast.25) | data formatting | bytes 18874368 | tf_op jit(solution)/shard_map/stack;reshape | solution.py:195
  474.0 0.0 copy-start
  474.0 13.3 %copy.16 = bf16[3,1,128,48,256]{2,4,3,0,1:T(8,128)(2,1)} copy(bf16[3,1,128,48,256]{4,3,2,0,1:T(8,128)(2,1)} %bitcast.23) | data formatting | bytes 18874368 | tf_op jit(solution)/shard_map/stack;reshape | solution.py:195
  487.3 0.0 copy-done
  487.3 9.8 %convert_bitcast_fusion = bf16[3,1,128,48,256]{2,4,3,0,1:T(8,128)(2,1)} fusion(bf16[3,128,48,256]{3,2,1,0:T(8,128)(2,1)} %bitcast.22, f32[128,128]{1,0:T(8,128)S(1)} %copy-done), kind=kOutput, calls=%fused_computation.4 | convolution fusion | flops 1212694528 | bytes 18939904 | tf_op jit(solution)/shard_map/czyx,zw->cwyx/dot_general | solution.py:192
  497.1 19.6 %pad_maximum_fusion = bf16[3,3,128,48,256]{2,4,3,0,1:T(8,128)(2,1)} fusion(bf16[3,1,128,48,256]{2,4,3,0,1:T(8,128)(2,1)} %convert_bitcast_fusion, bf16[3,1,128,48,256]{2,4,3,0,1:T(8,128)(2,1)} %copy.16, bf16[3,1,128,48,256]{2,4,3,0,1:T(8,128)(2,1)} %copy.15), kind=kLoop, calls=%fused_computation | loop fusion | flops 28311552 | bytes 56623104 | tf_op jit(solution)/shard_map/stack | solution.py:195
  516.7 38.2 %copy.17 = bf16[3,3,128,48,256]{4,3,2,1,0:T(8,128)(2,1)} copy(bf16[3,3,128,48,256]{2,4,3,0,1:T(8,128)(2,1)} %pad_maximum_fusion) | data formatting | bytes 56623104 | tf_op jit(solution)/shard_map/stack | solution.py:195
Async XLA Ops:
  474.0 13.3 %copy-start = (f32[128,128]{1,0:T(8,128)S(1)}, f32[128,128]{1,0:T(8,128)}, u32[]{:S(2)}) copy-start(f32[128,128]{1,0:T(8,128)} %param.8) | copy-start | bytes 196612

commit v2 on v1

v2 whole, which is shorter than its diff:
```python
import functools

import jax
import jax.numpy as jnp
from jax import lax
from jax.experimental import pallas as pl
from jax.experimental.pallas import tpu as pltpu
from jax.sharding import PartitionSpec as P

MESH = pl.DeviceIdType.MESH
HALVES = 2


def kernel(
    rows, cols, halves, v_ref, yop_ref, metric_ref, zop_ref, xop_ref, vz_ref, g_ref,
    ypen, ay, xpen, blocks, stage, yop, kron,
    row_v_s, row_v_r, col_v_s, col_v_r, col_y_s, col_y_r, row_f_s, row_f_r, row_x_s, row_x_r, own_sem, stage_sem,
):
    r, c = lax.axis_index("row"), lax.axis_index("col")
    chunks, _, k, zh, yc, xb = ypen.shape
    zb, nz = zh * halves, zh * halves * cols
    group = 16 if yc % 16 == 0 else 8

    def place(q):
        return q // halves, pl.ds((q % halves) * zh, zh)

    def load(q):
        comp, zs = place(q)
        return pltpu.make_async_copy(v_ref.at[comp, zs], stage.at[q % 2], stage_sem.at[q % 2])

    load(0).start()
    load(1).start()

    barrier = pltpu.get_barrier_semaphore()
    for d in range(1, rows):
        pl.semaphore_signal(barrier, inc=1, device_id=(lax.rem(r + d, rows), c), device_id_type=MESH)
    for d in range(1, cols):
        pl.semaphore_signal(barrier, inc=1, device_id=(r, lax.rem(c + d, cols)), device_id_type=MESH)
    pl.semaphore_wait(barrier, rows + cols - 2)

    def remote(src, dst, send, recv, target):
        return pltpu.make_async_remote_copy(
            src_ref=src, dst_ref=dst, send_sem=send, recv_sem=recv, device_id=target, device_id_type=MESH
        )

    def row_family(q, source, dst, send, recv, own):
        others = []
        for d in range(1, rows):
            t = lax.rem(r + d, rows)
            others.append(remote(source(t), dst, send.at[q, d - 1], recv.at[q, d - 1], (t, c)))
        return others, pltpu.make_async_copy(source(r), dst, own_sem.at[own, q])

    def col_family(q, source, dst, send, recv, own):
        others = []
        for d in range(1, cols):
            t = lax.rem(c + d, cols)
            others.append(remote(source(t), dst, send.at[q, d - 1], recv.at[q, d - 1], (r, t)))
        return others, pltpu.make_async_copy(source(c), dst, own_sem.at[own, q])

    def row_v(q):
        return row_family(q, lambda t: blocks.at[q, t], ypen.at[q, r], row_v_s, row_v_r, 0)

    def col_v(q):
        comp, zs = place(q)
        dst = vz_ref.at[comp, c // k, c % k, zs]
        return col_family(q, lambda t: ypen.at[q, t // k, t % k], dst, col_v_s, col_v_r, 1)

    def col_y(q):
        comp, zs = place(q)
        dst = g_ref.at[comp, 1, c // k, c % k, zs]
        return col_family(q, lambda t: ay.at[q, t // k, t % k], dst, col_y_s, col_y_r, 2)

    def row_f(q):
        comp, zs = place(q)
        return row_family(q, lambda t: vz_ref.at[comp, t, :, zs], xpen.at[q, r], row_f_s, row_f_r, 3)

    def row_x(q):
        comp, zs = place(q)
        return row_family(q, lambda t: blocks.at[q, t], g_ref.at[comp, 0, r, :, zs], row_x_s, row_x_r, 4)

    def field_in(q):
        comp, zs = place(q)
        return pltpu.make_async_copy(vz_ref.at[comp, :, :, zs], ypen.at[q], own_sem.at[5, q])

    def along_z_out(q):
        comp, zs = place(q)
        return pltpu.make_async_copy(xpen.at[q], g_ref.at[comp, 2, :, :, zs], own_sem.at[6, q])

    def start(family, q):
        others, own = family(q)
        for copy in others:
            copy.start()
        own.start()

    def arrived(family, q):
        others, own = family(q)
        for copy in others:
            copy.wait_recv()
        own.wait()

    def sent(family, q):
        for copy in family(q)[0]:
            copy.wait_send()

    def flat(x, width):
        if yc % 16:
            return x.astype(jnp.float32).reshape(-1, width).astype(x.dtype)
        return x.reshape(-1, width)

    def cast(q):
        @pl.loop(0, zh)
        def _(z):
            for part in range(k):
                for w in range(rows):
                    field = stage[q % 2, z, pl.ds(part * yc, yc), pl.ds(w * xb, xb)]
                    blocks[q, w, part, z] = field.astype(blocks.dtype)

    def along_y(q):
        @pl.loop(0, zh)
        def _(z):
            field = flat(ypen[q, :, :, z], xb)
            product = jnp.dot(yop[...], field, preferred_element_type=jnp.float32)
            ay[q, :, :, z] = product.reshape(rows, k, yc, xb).astype(ay.dtype)

    def along_x(q):
        field = jnp.concatenate([flat(xpen[q, j], xb) for j in range(rows)], axis=1)

        @pl.loop(0, rows)
        def _(w):
            operator = xop_ref[:, pl.ds(pl.multiple_of(w * xb, 128), xb)]
            product = jnp.dot(field, operator, preferred_element_type=jnp.float32)
            blocks[q, w] = product.reshape(k, zh, yc, xb).astype(blocks.dtype)

    def z_of(n):
        half, block = n // (nz // halves * group), n // (zh * group) % cols
        return block * zb + half * zh + n // group % zh

    def make_kron():
        wide, tall = nz // halves * group, zh * group * k

        @pl.loop(0, halves * rows)
        def _(m):
            at = lax.broadcasted_iota(jnp.int32, (tall, nz), 0) + m * tall
            pick = jnp.where(z_of(at) == lax.broadcasted_iota(jnp.int32, (tall, nz), 1), 1.0, 0.0)
            line = lax.dot_general(
                pick.astype(kron.dtype), zop_ref[...].astype(kron.dtype), (((1,), (1,)), ((), ())),
                preferred_element_type=jnp.float32,
            ).astype(kron.dtype)
            for h in range(halves):
                across = lax.broadcasted_iota(jnp.int32, (nz, wide), 1) + h * wide
                spread = jnp.where(z_of(across) == lax.broadcasted_iota(jnp.int32, (nz, wide), 0), 1.0, 0.0)
                full = jnp.dot(line, spread.astype(kron.dtype), preferred_element_type=jnp.float32)
                down = lax.broadcasted_iota(jnp.int32, (tall, wide), 0) % group
                same = down == lax.broadcasted_iota(jnp.int32, (tall, wide), 1) % group
                kron[h, pl.ds(m * tall, tall)] = jnp.where(same, full, 0.0).astype(kron.dtype)

    def along_z(comp):
        tall = zh * group * k

        @pl.loop(0, halves * rows)
        def _(m):
            lines = []
            for g in range(yc // group):
                total = None
                for h in range(halves):
                    if yc % 16:
                        field = ypen[comp * halves + h].astype(jnp.float32)[:, :, :, g * group:(g + 1) * group]
                    else:
                        field = ypen[comp * halves + h, :, :, :, pl.ds(g * group, group)]
                    field = field.reshape(-1, xb).astype(kron.dtype)
                    part = jnp.dot(kron[h, pl.ds(m * tall, tall)], field, preferred_element_type=jnp.float32)
                    total = part if total is None else total + part
                lines.append(total.reshape(k, zh, group, xb))
            q = comp * halves + m // rows
            if yc % 16:
                xpen[q, m % rows] = jnp.concatenate(lines, axis=2).astype(xpen.dtype)
            else:
                for g, line in enumerate(lines):
                    xpen[q, m % rows, :, :, pl.ds(g * group, group)] = line.astype(xpen.dtype)

    @pl.loop(0, chunks)
    def _(q):
        load(q).wait()
        cast(q)

        @pl.when(q + 2 < chunks)
        def _():
            load(q + 2).start()

        start(row_v, q)

    yop[...] = (yop_ref[...] * metric_ref[...]).T.astype(yop.dtype)

    @pl.loop(0, chunks)
    def _(q):
        arrived(row_v, q)
        start(col_v, q)
        along_y(q)

    make_kron()

    def finish_x(q):
        sent(row_v, q)
        arrived(row_f, q)
        along_x(q)
        start(row_x, q)

    @pl.loop(0, chunks)
    def _(q):
        arrived(col_v, q)
        start(row_f, q)
        start(col_y, q)

        @pl.when(q > 0)
        def _():
            finish_x(q - 1)

    finish_x(chunks - 1)

    @pl.loop(0, chunks)
    def _(q):
        sent(col_v, q)
        field_in(q).start()

    @pl.loop(0, chunks // halves)
    def _(comp):
        for h in range(halves):
            field_in(comp * halves + h).wait()
        along_z(comp)
        for h in range(halves):
            along_z_out(comp * halves + h).start()

    @pl.loop(0, chunks)
    def _(q):
        arrived(row_x, q)
        arrived(col_y, q)
        along_z_out(q).wait()
        for family in (col_y, row_f, row_x):
            sent(family, q)


def shards(rows, cols, velocity, x_operator, y_operator, z_operator, y_metric):
    bf16 = jnp.bfloat16
    comps, zb, yb, nx = velocity.shape
    k = cols // rows
    yc, xb, ny, nz = yb // k, nx // rows, yb * rows, zb * cols
    halves = HALVES
    zh, chunks = zb // halves, comps * halves
    group = 16 if yc % 16 == 0 else 8

    buffer = pltpu.VMEM((chunks, rows, k, zh, yc, xb), bf16)
    row_sem = pltpu.SemaphoreType.DMA((chunks, rows - 1))
    col_sem = pltpu.SemaphoreType.DMA((chunks, cols - 1))
    work = comps * zb * yb * nx
    _, grads = pl.pallas_call(
        functools.partial(kernel, rows, cols, halves),
        out_shape=[
            jax.ShapeDtypeStruct((comps, rows, k, zb, yc, xb), bf16),
            jax.ShapeDtypeStruct((comps, 3, rows, k, zb, yc, xb), bf16),
        ],
        in_specs=[pl.BlockSpec(memory_space=pl.ANY)] + [pl.BlockSpec(memory_space=pltpu.VMEM)] * 4,
        out_specs=[pl.BlockSpec(memory_space=pl.ANY)] * 2,
        scratch_shapes=[
            buffer, buffer, buffer, buffer,
            pltpu.VMEM((2, zh, yb, nx), jnp.float32),
            pltpu.VMEM((ny, ny), bf16),
            pltpu.VMEM((halves, nz * group, nz // halves * group), bf16),
            row_sem, row_sem, col_sem, col_sem, col_sem, col_sem, row_sem, row_sem, row_sem, row_sem,
            pltpu.SemaphoreType.DMA((7, chunks)),
            pltpu.SemaphoreType.DMA((2,)),
        ],
        cost_estimate=pl.CostEstimate(
            flops=2 * work * (nx + ny + nz * group), bytes_accessed=14 * work, transcendentals=0
        ),
        compiler_params=pltpu.CompilerParams(
            collective_id=0, has_side_effects=True, vmem_limit_bytes=61 * 2**20
        ),
    )(velocity, y_operator, y_metric[None, :], z_operator, x_operator.astype(bf16))
    return grads.reshape(3 * comps, nz, yc, xb)


def solution(mesh):
    return jax.shard_map(
        functools.partial(shards, mesh.shape["row"], mesh.shape["col"]),
        mesh=mesh,
        in_specs=(P(None, "col", "row", None), P(), P(), P(), P()),
        out_specs=P(None, None, "col", "row"),
        check_vma=False,
    )
```

time: 557 us -> 458 us (0.82)
  local copies, waits for them, and re-layouts: 81.4 us -> 20.9 us
  other arithmetic: 31.1 us -> 3.83 us
  matrix products: 9.77 us -> 0 us
    another operation x3 -> x0, local copies, waits for them, and re-layouts: 64.8 us -> none  [shards(): return jnp.stack([gx, gy, gz], axis=1).reshape(3 * comps, cols * zb, yc, xb)]
    another operation x1 -> x0, other arithmetic: 19.6 us -> none  [shards(): return jnp.stack([gx, gy, gz], axis=1).reshape(3 * comps, cols * zb, yc, xb)]
    unnamed x4 -> x1, local copies, waits for them, and re-layouts: 4.64 us -> 19.7 us
    reshape x2 -> x0, local copies, waits for them, and re-layouts: 11.9 us -> none  [the longest x1 9.4 us: shards(): velocity.astype(bf16).reshape(comps, zb, k, yc, nx).transpose(0, 2, 1, 3, 4)]
    dot_general x1 -> x0, matrix products: 9.77 us -> none  [shards(): jnp.einsum('czyx,zw->cwyx', vz, z_operator.astype(bf16), preferred_elemen...]
    convert_element_type x2 -> x1, other arithmetic: 11.5 us -> 3.83 us  [shards(): x_operator.astype(bf16)]
where the time goes in v2:
time: 458 us; the launch traced here: 457 us
  Pallas kernels  432 us (94%)
  local copies, waits for them, and re-layouts  20.9 us (5%)
    pallas_call x1, Pallas kernels, shards(): pl.pallas_call(functools.partial(kernel, rows, cols, halves), out_shape=[...  432 us
    unnamed x1, local copies, waits for them, and re-layouts  19.7 us

profile of v2, /device:TPU:9, one launch (start us, length us, event | category | flops | bytes accessed | tf_op | source)
XLA Modules:
  0.0 457.2 jit_solution(11688758628201906426)
XLA Ops:
  0.0 1.2 broadcast_in_dim.3.metric_ref
  1.2 3.8 convert_element_type.3.xop_ref
  5.0 432.5 %shard_map.55 = (bf16[3,4,2,16,48,256]{5,4,3,2,1,0:T(8,128)(2,1)}, bf16[3,3,4,2,16,48,256]{6,5,4,3,2,1,0:T(8,128)(2,1)}) custom-call(f32[3,16,96,1024]{3,2,1,0:T(8,128)} %v_ref.1, f32[384,384]{1,0:T(8,128)} %yop_ref.1, f32[1,384]{1,0:T(1,128)} %broadcast_in_dim.3.metric_ref, f32[128,128]{1,0:T(8,128)} %zop_ref.1, bf16[1024,1024]{1,0:T(8,128)(2,1)} %convert_element_type.3.xop_ref), custom_call_target="tpu_custom_call" | custom-call | flops 32614907904 | bytes 66060288 | tf_op jit(solution)/shard_map/pallas_call | solution.py:255
  437.5 19.7 %copy.7 = bf16[9,128,48,256]{3,2,1,0:T(8,128)(2,1)} copy(bf16[9,128,48,256]{3,2,1,0:T(8,128)(2,1)} %bitcast.1) | data formatting | bytes 56623104

commit v3 on v2

--- a/solution.py
+++ b/solution.py
@@ -8,28 +8,36 @@
 from jax.sharding import PartitionSpec as P
 
 MESH = pl.DeviceIdType.MESH
-HALVES = 2
+PARTS = 4
 
 
 def kernel(
-    rows, cols, halves, v_ref, yop_ref, metric_ref, zop_ref, xop_ref, vz_ref, g_ref,
-    ypen, ay, xpen, blocks, stage, yop, kron,
+    rows, cols, parts, v_ref, xop_ref, yop_ref, metric_ref, zop_ref, vz_ref, g_ref,
+    ypen, ay, xpen, blocks, stage, xop_in, yop_in, xop, yop, kron,
     row_v_s, row_v_r, col_v_s, col_v_r, col_y_s, col_y_r, row_f_s, row_f_r, row_x_s, row_x_r, own_sem, stage_sem,
 ):
     r, c = lax.axis_index("row"), lax.axis_index("col")
     chunks, _, k, zh, yc, xb = ypen.shape
-    zb, nz = zh * halves, zh * halves * cols
+    zb, nz = zh * parts, zh * parts * cols
     group = 16 if yc % 16 == 0 else 8
 
     def place(q):
-        return q // halves, pl.ds((q % halves) * zh, zh)
+        return q // parts, pl.ds((q % parts) * zh, zh)
 
     def load(q):
         comp, zs = place(q)
         return pltpu.make_async_copy(v_ref.at[comp, zs], stage.at[q % 2], stage_sem.at[q % 2])
+
+    def load_operators():
+        return [
+            pltpu.make_async_copy(yop_ref, yop_in, stage_sem.at[2]),
+            pltpu.make_async_copy(xop_ref, xop_in, stage_sem.at[3]),
+        ]
 
     load(0).start()
     load(1).start()
+    for copy in load_operators():
+        copy.start()
 
     barrier = pltpu.get_barrier_semaphore()
     for d in range(1, rows):
@@ -127,18 +135,19 @@
 
         @pl.loop(0, rows)
         def _(w):
-            operator = xop_ref[:, pl.ds(pl.multiple_of(w * xb, 128), xb)]
+            operator = xop[:, pl.ds(pl.multiple_of(w * xb, 128), xb)]
             product = jnp.dot(field, operator, preferred_element_type=jnp.float32)
             blocks[q, w] = product.reshape(k, zh, yc, xb).astype(blocks.dtype)
 
     def z_of(n):
-        half, block = n // (nz // halves * group), n // (zh * group) % cols
+        half, block = n // (nz // parts * group), n // (zh * group) % cols
         return block * zb + half * zh + n // group % zh
 
     def make_kron():
-        wide, tall = nz // halves * group, zh * group * k
-
-        @pl.loop(0, halves * rows)
+        wide = nz // parts * group
+        tall = wide
+
+        @pl.loop(0, parts)
         def _(m):
             at = lax.broadcasted_iota(jnp.int32, (tall, nz), 0) + m * tall
             pick = jnp.where(z_of(at) == lax.broadcasted_iota(jnp.int32, (tall, nz), 1), 1.0, 0.0)
@@ -146,7 +155,7 @@
                 pick.astype(kron.dtype), zop_ref[...].astype(kron.dtype), (((1,), (1,)), ((), ())),
                 preferred_element_type=jnp.float32,
             ).astype(kron.dtype)
-            for h in range(halves):
+            for h in range(parts):
                 across = lax.broadcasted_iota(jnp.int32, (nz, wide), 1) + h * wide
                 spread = jnp.where(z_of(across) == lax.broadcasted_iota(jnp.int32, (nz, wide), 0), 1.0, 0.0)
                 full = jnp.dot(line, spread.astype(kron.dtype), preferred_element_type=jnp.float32)
@@ -155,46 +164,59 @@
                 kron[h, pl.ds(m * tall, tall)] = jnp.where(same, full, 0.0).astype(kron.dtype)
 
     def along_z(comp):
-        tall = zh * group * k
-
-        @pl.loop(0, halves * rows)
+        tall = nz // parts * group
+
+        @pl.loop(0, parts)
         def _(m):
             lines = []
             for g in range(yc // group):
                 total = None
-                for h in range(halves):
+                for h in range(parts):
                     if yc % 16:
-                        field = ypen[comp * halves + h].astype(jnp.float32)[:, :, :, g * group:(g + 1) * group]
+                        field = ypen[comp * parts + h].astype(jnp.float32)[:, :, :, g * group:(g + 1) * group]
                     else:
-                        field = ypen[comp * halves + h, :, :, :, pl.ds(g * group, group)]
+                        field = ypen[comp * parts + h, :, :, :, pl.ds(g * group, group)]
                     field = field.reshape(-1, xb).astype(kron.dtype)
                     part = jnp.dot(kron[h, pl.ds(m * tall, tall)], field, preferred_element_type=jnp.float32)
                     total = part if total is None else total + part
-                lines.append(total.reshape(k, zh, group, xb))
-            q = comp * halves + m // rows
+                lines.append(total.reshape(rows, k, zh, group, xb))
+            q = comp * parts + m
             if yc % 16:
-                xpen[q, m % rows] = jnp.concatenate(lines, axis=2).astype(xpen.dtype)
+                xpen[q] = jnp.concatenate(lines, axis=3).astype(xpen.dtype)
             else:
                 for g, line in enumerate(lines):
-                    xpen[q, m % rows, :, :, pl.ds(g * group, group)] = line.astype(xpen.dtype)
+                    xpen[q, :, :, :, pl.ds(g * group, group)] = line.astype(xpen.dtype)
+
+    def pass_on(q):
+        arrived(row_v, q)
+        start(col_v, q)
 
     @pl.loop(0, chunks)
     def _(q):
         load(q).wait()
         cast(q)
+        start(row_v, q)
 
         @pl.when(q + 2 < chunks)
         def _():
             load(q + 2).start()
 
-        start(row_v, q)
-
-    yop[...] = (yop_ref[...] * metric_ref[...]).T.astype(yop.dtype)
-
-    @pl.loop(0, chunks)
-    def _(q):
-        arrived(row_v, q)
-        start(col_v, q)
+        @pl.when(q > 0)
+        def _():
+            pass_on(q - 1)
+
+    pass_on(chunks - 1)
+    for copy in load_operators():
+        copy.wait()
+    yop[...] = (yop_in[...] * metric_ref[...]).T.astype(yop.dtype)
+
+    @pl.loop(0, rows)
+    def _(w):
+        lines = pl.ds(w * xb, xb)
+        xop[lines] = xop_in[lines].astype(xop.dtype)
+
+    @pl.loop(0, chunks)
+    def _(q):
         along_y(q)
 
     make_kron()
@@ -222,13 +244,13 @@
         sent(col_v, q)
         field_in(q).start()
 
-    @pl.loop(0, chunks // halves)
+    @pl.loop(0, chunks // parts)
     def _(comp):
-        for h in range(halves):
-            field_in(comp * halves + h).wait()
+        for h in range(parts):
+            field_in(comp * parts + h).wait()
         along_z(comp)
-        for h in range(halves):
-            along_z_out(comp * halves + h).start()
+        for h in range(parts):
+            along_z_out(comp * parts + h).start()
 
     @pl.loop(0, chunks)
     def _(q):
@@ -244,8 +266,8 @@
     comps, zb, yb, nx = velocity.shape
     k = cols // rows
     yc, xb, ny, nz = yb // k, nx // rows, yb * rows, zb * cols
-    halves = HALVES
-    zh, chunks = zb // halves, comps * halves
+    parts = PARTS
+    zh, chunks = zb // parts, comps * parts
     group = 16 if yc % 16 == 0 else 8
 
     buffer = pltpu.VMEM((chunks, rows, k, zh, yc, xb), bf16)
@@ -253,21 +275,24 @@
     col_sem = pltpu.SemaphoreType.DMA((chunks, cols - 1))
     work = comps * zb * yb * nx
     _, grads = pl.pallas_call(
-        functools.partial(kernel, rows, cols, halves),
+        functools.partial(kernel, rows, cols, parts),
         out_shape=[
             jax.ShapeDtypeStruct((comps, rows, k, zb, yc, xb), bf16),
             jax.ShapeDtypeStruct((comps, 3, rows, k, zb, yc, xb), bf16),
         ],
-        in_specs=[pl.BlockSpec(memory_space=pl.ANY)] + [pl.BlockSpec(memory_space=pltpu.VMEM)] * 4,
+        in_specs=[pl.BlockSpec(memory_space=pl.ANY)] * 3 + [pl.BlockSpec(memory_space=pltpu.VMEM)] * 2,
         out_specs=[pl.BlockSpec(memory_space=pl.ANY)] * 2,
         scratch_shapes=[
             buffer, buffer, buffer, buffer,
             pltpu.VMEM((2, zh, yb, nx), jnp.float32),
+            pltpu.VMEM((nx, nx), jnp.float32),
+            pltpu.VMEM((ny, ny), jnp.float32),
+            pltpu.VMEM((nx, nx), bf16),
             pltpu.VMEM((ny, ny), bf16),
-            pltpu.VMEM((halves, nz * group, nz // halves * group), bf16),
+            pltpu.VMEM((parts, nz * group, nz // parts * group), bf16),
             row_sem, row_sem, col_sem, col_sem, col_sem, col_sem, row_sem, row_sem, row_sem, row_sem,
             pltpu.SemaphoreType.DMA((7, chunks)),
-            pltpu.SemaphoreType.DMA((2,)),
+            pltpu.SemaphoreType.DMA((4,)),
         ],
         cost_estimate=pl.CostEstimate(
             flops=2 * work * (nx + ny + nz * group), bytes_accessed=14 * work, transcendentals=0
@@ -275,7 +300,7 @@
         compiler_params=pltpu.CompilerParams(
             collective_id=0, has_side_effects=True, vmem_limit_bytes=61 * 2**20
         ),
-    )(velocity, y_operator, y_metric[None, :], z_operator, x_operator.astype(bf16))
+    )(velocity, x_operator, y_operator, y_metric[None, :], z_operator)
     return grads.reshape(3 * comps, nz, yc, xb)
 
 

time: 458 us -> 447 us (0.976)
  Pallas kernels: 432 us -> 426 us
    pallas_call x1, Pallas kernels: 432 us -> 426 us  [shards(): pl.pallas_call(functools.partial(kernel, rows, cols, parts), out_shape=[j...]
where the time goes in v3:
time: 447 us
  Pallas kernels  426 us (95%)
  local copies, waits for them, and re-layouts  20.9 us (5%)
    pallas_call x1, Pallas kernels, shards(): pl.pallas_call(functools.partial(kernel, rows, cols, parts), out_shape=[j...  426 us
    unnamed x1, local copies, waits for them, and re-layouts  19.7 us

profile of v3, /device:TPU:9, one launch (start us, length us, event | category | flops | bytes accessed | tf_op | source)
XLA Modules:
  0.0 447.1 jit_solution(6766430298162234893)
XLA Ops:
  0.0 1.2 broadcast_in_dim.3.metric_ref
  1.2 426.1 %shard_map.55 = (bf16[3,4,2,16,48,256]{5,4,3,2,1,0:T(8,128)(2,1)}, bf16[3,3,4,2,16,48,256]{6,5,4,3,2,1,0:T(8,128)(2,1)}) custom-call(f32[3,16,96,1024]{3,2,1,0:T(8,128)} %v_ref.1, f32[1024,1024]{1,0:T(8,128)} %xop_ref.1, f32[384,384]{1,0:T(8,128)} %yop_ref.1, f32[1,384]{1,0:T(1,128)} %broadcast_in_dim.3.metric_ref, f32[128,128]{1,0:T(8,128)} %zop_ref.1), custom_call_target="tpu_custom_call" | custom-call | flops 32614907904 | bytes 66060288 | tf_op jit(solution)/shard_map/pallas_call | solution.py:277
  427.4 19.7 %copy.7 = bf16[9,128,48,256]{3,2,1,0:T(8,128)(2,1)} copy(bf16[9,128,48,256]{3,2,1,0:T(8,128)(2,1)} %bitcast.1) | data formatting | bytes 56623104

commit v4 on v3

--- a/solution.py
+++ b/solution.py
@@ -9,6 +9,7 @@
 
 MESH = pl.DeviceIdType.MESH
 PARTS = 4
+AHEAD = 3
 
 
 def kernel(
@@ -191,8 +192,7 @@
         arrived(row_v, q)
         start(col_v, q)
 
-    @pl.loop(0, chunks)
-    def _(q):
+    def begin(q):
         load(q).wait()
         cast(q)
         start(row_v, q)
@@ -200,26 +200,6 @@
         @pl.when(q + 2 < chunks)
         def _():
             load(q + 2).start()
-
-        @pl.when(q > 0)
-        def _():
-            pass_on(q - 1)
-
-    pass_on(chunks - 1)
-    for copy in load_operators():
-        copy.wait()
-    yop[...] = (yop_in[...] * metric_ref[...]).T.astype(yop.dtype)
-
-    @pl.loop(0, rows)
-    def _(w):
-        lines = pl.ds(w * xb, xb)
-        xop[lines] = xop_in[lines].astype(xop.dtype)
-
-    @pl.loop(0, chunks)
-    def _(q):
-        along_y(q)
-
-    make_kron()
 
     def finish_x(q):
         sent(row_v, q)
@@ -227,16 +207,53 @@
         along_x(q)
         start(row_x, q)
 
+    @pl.loop(0, AHEAD + 1)
+    def _(q):
+        begin(q)
+
+        @pl.when(q > 0)
+        def _():
+            pass_on(q - 1)
+
+    for copy in load_operators():
+        copy.wait()
+    yop[...] = (yop_in[...] * metric_ref[...][None, :]).T.astype(yop.dtype)
+
+    @pl.loop(0, rows)
+    def _(w):
+        lines = pl.ds(w * xb, xb)
+        xop[lines] = xop_in[lines].astype(xop.dtype)
+
+    make_kron()
+
     @pl.loop(0, chunks)
     def _(q):
+        @pl.when(q + AHEAD + 1 < chunks)
+        def _():
+            begin(q + AHEAD + 1)
+
         arrived(col_v, q)
+
+        @pl.when(q + AHEAD < chunks)
+        def _():
+            pass_on(q + AHEAD)
+
         start(row_f, q)
+        along_y(q)
+
+        @pl.when(q + AHEAD >= chunks)
+        def _():
+            start(col_y, q + AHEAD - chunks)
+
+        @pl.when(q >= 2)
+        def _():
+            finish_x(q - 2)
+
+    @pl.loop(AHEAD, chunks)
+    def _(q):
         start(col_y, q)
 
-        @pl.when(q > 0)
-        def _():
-            finish_x(q - 1)
-
+    finish_x(chunks - 2)
     finish_x(chunks - 1)
 
     @pl.loop(0, chunks)
@@ -300,7 +317,7 @@
         compiler_params=pltpu.CompilerParams(
             collective_id=0, has_side_effects=True, vmem_limit_bytes=61 * 2**20
         ),
-    )(velocity, x_operator, y_operator, y_metric[None, :], z_operator)
+    )(velocity, x_operator, y_operator, y_metric, z_operator)
     return grads.reshape(3 * comps, nz, yc, xb)
 
 

time: 447 us -> 459 us (1.027)
  Pallas kernels: 426 us -> 439 us
    pallas_call x1, Pallas kernels: 426 us -> 439 us  [shards(): pl.pallas_call(functools.partial(kernel, rows, cols, parts), out_shape=[j...]
where the time goes in v4:
time: 459 us; the launch traced here: 458 us
  Pallas kernels  439 us (96%)
  local copies, waits for them, and re-layouts  19.7 us (4%)
    pallas_call x1, Pallas kernels, shards(): pl.pallas_call(functools.partial(kernel, rows, cols, parts), out_shape=[j...  439 us
    unnamed x1, local copies, waits for them, and re-layouts  19.7 us

profile of v4, /device:TPU:9, one launch (start us, length us, event | category | flops | bytes accessed | tf_op | source)
XLA Modules:
  0.0 458.3 jit_solution(10380713282155795858)
XLA Ops:
  0.0 438.6 %shard_map.55 = (bf16[3,4,2,16,48,256]{5,4,3,2,1,0:T(8,128)(2,1)}, bf16[3,3,4,2,16,48,256]{6,5,4,3,2,1,0:T(8,128)(2,1)}) custom-call(f32[3,16,96,1024]{3,2,1,0:T(8,128)} %v_ref.1, f32[1024,1024]{1,0:T(8,128)} %xop_ref.1, f32[384,384]{1,0:T(8,128)} %yop_ref.1, f32[384]{0:T(512)} %metric_ref.1, f32[128,128]{1,0:T(8,128)} %zop_ref.1), custom_call_target="tpu_custom_call" | custom-call | flops 32614907904 | bytes 66060288 | tf_op jit(solution)/shard_map/pallas_call | solution.py:294
  438.6 19.7 %copy.7 = bf16[9,128,48,256]{3,2,1,0:T(8,128)(2,1)} copy(bf16[9,128,48,256]{3,2,1,0:T(8,128)(2,1)} %bitcast.1) | data formatting | bytes 56623104

commit v5 on v3

--- a/solution.py
+++ b/solution.py
@@ -58,9 +58,16 @@
             others.append(remote(source(t), dst, send.at[q, d - 1], recv.at[q, d - 1], (t, c)))
         return others, pltpu.make_async_copy(source(r), dst, own_sem.at[own, q])
 
+    far_first = sorted(range(1, cols), key=lambda d: abs(d - cols // 2))
+    col_order = []
+    while far_first:
+        col_order.append(far_first.pop(0))
+        if far_first:
+            col_order.append(far_first.pop())
+
     def col_family(q, source, dst, send, recv, own):
         others = []
-        for d in range(1, cols):
+        for d in col_order:
             t = lax.rem(c + d, cols)
             others.append(remote(source(t), dst, send.at[q, d - 1], recv.at[q, d - 1], (r, t)))
         return others, pltpu.make_async_copy(source(c), dst, own_sem.at[own, q])
@@ -208,7 +215,7 @@
     pass_on(chunks - 1)
     for copy in load_operators():
         copy.wait()
-    yop[...] = (yop_in[...] * metric_ref[...]).T.astype(yop.dtype)
+    yop[...] = (yop_in[...] * metric_ref[...][None, :]).T.astype(yop.dtype)
 
     @pl.loop(0, rows)
     def _(w):
@@ -300,7 +307,7 @@
         compiler_params=pltpu.CompilerParams(
             collective_id=0, has_side_effects=True, vmem_limit_bytes=61 * 2**20
         ),
-    )(velocity, x_operator, y_operator, y_metric[None, :], z_operator)
+    )(velocity, x_operator, y_operator, y_metric, z_operator)
     return grads.reshape(3 * comps, nz, yc, xb)
 
 

time: 447 us -> 446 us (level)
  no operation moved by 1% of the time
where the time goes in v5:
time: 446 us
  Pallas kernels  426 us (96%)
  local copies, waits for them, and re-layouts  19.7 us (4%)
    pallas_call x1, Pallas kernels, shards(): pl.pallas_call(functools.partial(kernel, rows, cols, parts), out_shape=[j...  426 us
    unnamed x1, local copies, waits for them, and re-layouts  19.7 us

profile of v5, /device:TPU:9, one launch (start us, length us, event | category | flops | bytes accessed | tf_op | source)
XLA Modules:
  0.0 446.2 jit_solution(2916817678772796963)
XLA Ops:
  0.0 426.5 %shard_map.55 = (bf16[3,4,2,16,48,256]{5,4,3,2,1,0:T(8,128)(2,1)}, bf16[3,3,4,2,16,48,256]{6,5,4,3,2,1,0:T(8,128)(2,1)}) custom-call(f32[3,16,96,1024]{3,2,1,0:T(8,128)} %v_ref.1, f32[1024,1024]{1,0:T(8,128)} %xop_ref.1, f32[384,384]{1,0:T(8,128)} %yop_ref.1, f32[384]{0:T(512)} %metric_ref.1, f32[128,128]{1,0:T(8,128)} %zop_ref.1), custom_call_target="tpu_custom_call" | custom-call | flops 32614907904 | bytes 66060288 | tf_op jit(solution)/shard_map/pallas_call | solution.py:284
  426.5 19.7 %copy.7 = bf16[9,128,48,256]{3,2,1,0:T(8,128)(2,1)} copy(bf16[9,128,48,256]{3,2,1,0:T(8,128)(2,1)} %bitcast.1) | data formatting | bytes 56623104
